TPU v7x, 32 devices: a whole 2x2x4 slice. The times are simulated.
32 devices in a mesh: level: 8 (over z, x), sample: 4 (over y, core).
Axes of the slice: x: 2, y: 2, z: 4, core: 2. Of those that a mesh axis runs over, the one named last changes fastest.
Arguments:
- samples: bfloat16 [32768, 512], P('level', 'sample'), may hold values from -6 to 6
- sketch: bfloat16 [2, 128, 256], replicated, may hold values from -0.375 to 0.375
Outputs:
- far_factors: float32 [128, 128, 128], P('level')
- near_factors: float32 [64, 128, 128], P('level')
- basis_rows: float32 [8192, 512], P('level', 'sample')
All inputs are finite; a program needn't handle non-finite values.
Results may differ from a plain program's by a relative error of at most 0.0031.
Values may be sent and summed in bfloat16 or wider, within the bound.
A program may use at most 64 MiB of HBM per device.

v0:
```python
import math

import jax
import jax.numpy as jnp
from jax import lax
from jax.sharding import PartitionSpec as P

SAMPLES = 512


def partner(value, axis, distance):
    mask = 2**distance
    pairs = [(source, source ^ mask) for source in range(lax.axis_size(axis))]
    return lax.ppermute(value, axis, pairs)


def split_half(rows, bit):
    count = rows.shape[0] // 2
    upper = lax.axis_index("level") // (1 << bit) % 2
    kept = lax.dynamic_slice_in_dim(rows, upper * count, count, 0)
    given = lax.dynamic_slice_in_dim(rows, (1 - upper) * count, count, 0)
    return (kept, given, upper)


def solve_box(factor_box, block_box):
    return jax.scipy.linalg.solve_triangular(factor_box, block_box, lower=True)


def batch_product(first, second):
    return jnp.einsum("brs,bst->brt", first, second, precision=lax.Precision.HIGHEST)


def factor_inverse(gram):
    order = gram.shape[1]
    if order <= 32:
        factor = jnp.linalg.cholesky(gram)
        eye_block = jnp.broadcast_to(jnp.eye(order, dtype=jnp.float32), gram.shape)
        inverse = jax.vmap(solve_box)(factor, eye_block)
        return (factor, inverse)
    middle = order // 2
    top_factor, top_inverse = factor_inverse(gram[:, :middle, :middle])
    lower_left = batch_product(gram[:, middle:, :middle], jnp.swapaxes(top_inverse, 1, 2))
    schur = gram[:, middle:, middle:] - batch_product(lower_left, jnp.swapaxes(lower_left, 1, 2))
    bottom_factor, bottom_inverse = factor_inverse(schur)
    inverse_left = -batch_product(batch_product(bottom_inverse, lower_left), top_inverse)
    zeros_block = jnp.zeros((gram.shape[0], middle, order - middle), jnp.float32)
    factor = jnp.concatenate(
        (
            jnp.concatenate((top_factor, zeros_block), axis=2),
            jnp.concatenate((lower_left, bottom_factor), axis=2),
        ),
        axis=1,
    )
    inverse = jnp.concatenate(
        (
            jnp.concatenate((top_inverse, zeros_block), axis=2),
            jnp.concatenate((inverse_left, bottom_inverse), axis=2),
        ),
        axis=1,
    )
    return (factor, inverse)


def compress(kept, received, upper, sketch_level):
    rank = sketch_level.shape[0]
    columns = kept.shape[1]
    boxes = kept.shape[0] // rank
    flag = upper == 1
    lower_rows = jnp.where(flag, received, kept).reshape(boxes, rank, columns)
    upper_rows = jnp.where(flag, kept, received).reshape(boxes, rank, columns)
    projected = jnp.einsum(
        "rm,bmc->brc", sketch_level[:, :rank], lower_rows, preferred_element_type=jnp.float32
    )
    projected = projected + jnp.einsum(
        "rm,bmc->brc", sketch_level[:, rank:], upper_rows, preferred_element_type=jnp.float32
    )
    partial_gram = jnp.einsum("brc,bsc->brs", projected, projected, precision=lax.Precision.HIGHEST)
    gram = lax.psum(partial_gram, "sample")
    factor, inverse = factor_inverse(gram)
    solved = jnp.einsum(
        "brs,bsc->brc", inverse, projected, precision=lax.Precision.HIGHEST
    ) * math.sqrt(SAMPLES)
    return (factor, solved.reshape(boxes * rank, columns))


def shards(samples, sketch):
    far_bit = lax.axis_size("level").bit_length() - 2
    kept, given, upper = split_half(samples, far_bit)
    received = partner(given, "level", far_bit)
    far_factors, first_rows = compress(kept, received, upper, sketch[0])
    first_rows = first_rows.astype(jnp.bfloat16)
    kept, given, upper = split_half(first_rows, 0)
    received = partner(given, "level", 0)
    near_factors, basis_rows = compress(kept, received, upper, sketch[1])
    return (far_factors, near_factors, basis_rows)


def solution(mesh):
    return jax.shard_map(
        shards,
        mesh=mesh,
        in_specs=(P("level", "sample"), P()),
        out_specs=(P("level", None, None), P("level", None, None), P("level", "sample")),
        check_vma=False,
    )
```

profile of v0, /device:TPU:0, one launch (start us, length us, event | category | flops | bytes accessed | tf_op | source)
XLA Modules:
  0.0 682.3 jit_solution(6018807062260853348)
XLA Ops:
  7.3 1.2 constant_dynamic-slice_fusion.1
  8.4 4.1 collective-permute-start
  13.4 22.3 %collective-permute-done = bf16[2048,128]{1,0:T(8,128)(2,1)S(1)} collective-permute-done((bf16[2048,128]{1,0:T(8,128)(2,1)S(1)}, bf16[2048,128]{1,0:T(8,128)(2,1)S(1)}, u32[]{:S(2)}, u32[]{:S(2)}) %collective-permute-start) | collective-permute-done | bytes 524320 | tf_op jit(solution)/shard_map/ppermute | solution.py:14
  36.6 2.8 fusion.96
  39.7 37.2 %all-reduce.15.cloned.1.call-done = f32[16,128,128]{1,2,0:T(8,128)} async-done(((f32[16,128,128]{1,2,0:T(8,128)}), f32[16,128,128]{1,2,0:T(8,128)}) %all-reduce.15.cloned.1.call-update) | async-done | bytes 1048592 | tf_op jit(solution)/shard_map/psum | solution.py:78
  77.9 1.1 fusion.60
  79.0 46.9 %custom-call.24 = f32[16,32,32]{2,1,0:T(8,128)S(1)} custom-call(f32[16,32,32]{2,1,0:T(8,128)S(1)} %fusion.60), custom_call_target="Cholesky" | custom-call | tf_op jit(solution)/shard_map/jit(cholesky)/cholesky | solution.py:36
  126.9 39.4 %custom-call.25 = f32[16,1,32,32]{2,3,1,0:T(8,128)S(1)} custom-call(f32[16,1,32,32]{3,2,1,0:T(8,128)S(1)} %get-tuple-element.21), custom_call_target="InvertDiagBlocksLowerTriangular" | custom-call | tf_op jit(solution)/shard_map/vmap(jit(_solve_triangular))/triangular_solve | solution.py:26
  168.4 46.9 %custom-call.26 = f32[16,32,32]{2,1,0:T(8,128)S(1)} custom-call(f32[16,32,32]{2,1,0:T(8,128)S(1)} %fusion.57), custom_call_target="Cholesky" | custom-call | tf_op jit(solution)/shard_map/jit(cholesky)/cholesky | solution.py:36
  216.3 39.4 %custom-call.27 = f32[16,1,32,32]{2,3,1,0:T(8,128)S(1)} custom-call(f32[16,1,32,32]{3,2,1,0:T(8,128)S(1)} %get-tuple-element.19), custom_call_target="InvertDiagBlocksLowerTriangular" | custom-call | tf_op jit(solution)/shard_map/vmap(jit(_solve_triangular))/triangular_solve | solution.py:26
  257.9 1.2 fusion.16
  260.2 46.9 %custom-call.28 = f32[16,32,32]{2,1,0:T(8,128)S(1)} custom-call(f32[16,32,32]{2,1,0:T(8,128)S(1)} %fusion.54), custom_call_target="Cholesky" | custom-call | tf_op jit(solution)/shard_map/jit(cholesky)/cholesky | solution.py:36
  308.1 39.4 %custom-call.29 = f32[16,1,32,32]{2,3,1,0:T(8,128)S(1)} custom-call(f32[16,1,32,32]{3,2,1,0:T(8,128)S(1)} %get-tuple-element.17), custom_call_target="InvertDiagBlocksLowerTriangular" | custom-call | tf_op jit(solution)/shard_map/vmap(jit(_solve_triangular))/triangular_solve | solution.py:26
  348.9 1.2 convolution_subtract_fusion.2
  350.1 1.1 copy.106
  352.0 47.6 %custom-call.30 = f32[16,32,32]{2,1,0:T(8,128)S(1)} custom-call(f32[16,32,32]{2,1,0:T(8,128)} %fusion.51), custom_call_target="Cholesky" | custom-call | tf_op jit(solution)/shard_map/jit(cholesky)/cholesky | solution.py:36
  400.6 39.6 %custom-call.31 = f32[16,1,32,32]{2,3,1,0:T(8,128)S(1)} custom-call(f32[16,1,32,32]{3,2,1,0:T(8,128)S(1)} %get-tuple-element.15), custom_call_target="InvertDiagBlocksLowerTriangular" | custom-call | tf_op jit(solution)/shard_map/vmap(jit(_solve_triangular))/triangular_solve | solution.py:26
  443.0 2.4 fusion
  445.4 1.5 collective-permute-start.1
  446.9 6.4 collective-permute-done.1
  453.9 1.8 fusion.99
  457.8 1.3 fusion.3
  459.0 30.5 %all-reduce.17.cloned.1.call-done = f32[8,128,128]{1,2,0:T(8,128)} async-done(((f32[8,128,128]{1,2,0:T(8,128)}), f32[8,128,128]{1,2,0:T(8,128)}) %all-reduce.17.cloned.1.call-update) | async-done | bytes 524304 | tf_op jit(solution)/shard_map/psum | solution.py:78
  491.5 23.4 %custom-call.32 = f32[8,32,32]{2,1,0:T(8,128)S(1)} custom-call(f32[8,32,32]{2,1,0:T(8,128)S(1)} %fusion.76), custom_call_target="Cholesky" | custom-call | tf_op jit(solution)/shard_map/jit(cholesky)/cholesky | solution.py:36
  515.2 19.7 %custom-call.33 = f32[8,1,32,32]{2,3,1,0:T(8,128)S(1)} custom-call(f32[8,1,32,32]{3,2,1,0:T(8,128)S(1)} %get-tuple-element.13), custom_call_target="InvertDiagBlocksLowerTriangular" | custom-call | tf_op jit(solution)/shard_map/vmap(jit(_solve_triangular))/triangular_solve | solution.py:26
  536.3 23.4 %custom-call.34 = f32[8,32,32]{2,1,0:T(8,128)S(1)} custom-call(f32[8,32,32]{2,1,0:T(8,128)S(1)} %fusion.73), custom_call_target="Cholesky" | custom-call | tf_op jit(solution)/shard_map/jit(cholesky)/cholesky | solution.py:36
  560.0 19.7 %custom-call.35 = f32[8,1,32,32]{2,3,1,0:T(8,128)S(1)} custom-call(f32[8,1,32,32]{3,2,1,0:T(8,128)S(1)} %get-tuple-element.11), custom_call_target="InvertDiagBlocksLowerTriangular" | custom-call | tf_op jit(solution)/shard_map/vmap(jit(_solve_triangular))/triangular_solve | solution.py:26
  582.2 23.4 %custom-call.36 = f32[8,32,32]{2,1,0:T(8,128)S(1)} custom-call(f32[8,32,32]{2,1,0:T(8,128)S(1)} %fusion.70), custom_call_target="Cholesky" | custom-call | tf_op jit(solution)/shard_map/jit(cholesky)/cholesky | solution.py:36
  605.9 19.9 %custom-call.37 = f32[8,1,32,32]{2,3,1,0:T(8,128)S(1)} custom-call(f32[8,1,32,32]{3,2,1,0:T(8,128)S(1)} %get-tuple-element.9), custom_call_target="InvertDiagBlocksLowerTriangular" | custom-call | tf_op jit(solution)/shard_map/vmap(jit(_solve_triangular))/triangular_solve | solution.py:26
  627.1 23.4 %custom-call.38 = f32[8,32,32]{2,1,0:T(8,128)S(1)} custom-call(f32[8,32,32]{2,1,0:T(8,128)S(1)} %fusion.67), custom_call_target="Cholesky" | custom-call | tf_op jit(solution)/shard_map/jit(cholesky)/cholesky | solution.py:36
  650.8 19.7 %custom-call.39 = f32[8,1,32,32]{2,3,1,0:T(8,128)S(1)} custom-call(f32[8,1,32,32]{3,2,1,0:T(8,128)S(1)} %get-tuple-element.6), custom_call_target="InvertDiagBlocksLowerTriangular" | custom-call | tf_op jit(solution)/shard_map/vmap(jit(_solve_triangular))/triangular_solve | solution.py:26
  672.3 2.1 convolution_multiply_fusion.1
  (112 shorter events, 30.9 us)
Async XLA Ops:
  7.2 28.5 %copy-start.6 = (bf16[4096,128]{1,0:T(8,128)(2,1)S(1)}, bf16[4096,128]{1,0:T(8,128)(2,1)}, u32[]{:S(2)}) copy-start(bf16[4096,128]{1,0:T(8,128)(2,1)} %param.8) | copy-start | bytes 3145732
  7.2 69.6 %all-reduce.15.cloned.1.call-start = ((), (), s32[]{:S(2)}) async-start(), calls=%async_computation | async-start | bytes 2097152 | tf_op jit(solution)/shard_map/psum | solution.py:78
  8.4 27.3 %collective-permute-start = (bf16[2048,128]{1,0:T(8,128)(2,1)S(1)}, bf16[2048,128]{1,0:T(8,128)(2,1)S(1)}, u32[]{:S(2)}, u32[]{:S(2)}) collective-permute-start(bf16[2048,128]{1,0:T(8,128)(2,1)S(1)} %constant_dynamic-slice_fusion.1), channel_id=1, source_target_pairs={{0,16},{4,20},{8,24},{12,28},{16,0},{20,4},{24,8},{28,12},{1,17},{... | collective-permute-start | bytes 1572872 | tf_op jit(solution)/shard_map/ppermute | solution.py:14
  39.4 450.1 %all-reduce.17.cloned.1.call-start = ((), (), s32[]{:S(2)}) async-start(), calls=%async_computation.1 | async-start | bytes 1048576 | tf_op jit(solution)/shard_map/psum | solution.py:78
  77.9 89.0 %copy-start = (f32[16,128,128]{1,2,0:T(8,128)S(1)}, f32[16,128,128]{1,2,0:T(8,128)}, u32[]{:S(2)}) copy-start(f32[16,128,128]{1,2,0:T(8,128)} %all-reduce.15.cloned.1.call-done) | copy-start | bytes 3145732
  256.7 1.2 copy-start.1
  350.1 1.2 copy-start.2
  445.4 7.9 %collective-permute-start.1 = (bf16[1024,128]{1,0:T(8,128)(2,1)S(1)}, bf16[1024,128]{1,0:T(8,128)(2,1)S(1)}, u32[]{:S(2)}, u32[]{:S(2)}) collective-permute-start(bf16[1024,128]{1,0:T(8,128)(2,1)S(1)} %constant_dynamic-slice_fusion), channel_id=1, source_target_pairs={{0,4},{4,0},{8,12},{12,8},{16,20},{20,16},{24,28},{28,24},{1,5},{5... | collective-permute-start | bytes 786440 | tf_op jit(solution)/shard_map/ppermute | solution.py:14
  455.7 0.9 copy-start.4
  455.7 1.0 copy-start.5
  456.7 0.9 copy-start.7
  456.7 1.0 copy-start.8
  490.5 44.8 %copy-start.3 = (f32[8,128,128]{1,2,0:T(8,128)S(1)}, f32[8,128,128]{1,2,0:T(8,128)}, u32[]{:S(2)}) copy-start(f32[8,128,128]{1,2,0:T(8,128)} %all-reduce.17.cloned.1.call-done) | copy-start | bytes 1572868
Sparse Core Ops, SparseCore 0:
  39.5 37.2 all-reduce.14
  455.8 33.6 all-reduce.16
where the time goes:
time: 683 us; the launch traced here: 682 us
  other arithmetic  530 us (78%)
  waiting for transfers between devices  96.3 us (14%)
  matrix products  27.2 us (4%)
  between operations  14.7 us (2%)
  local copies, waits for them, and re-layouts  8.51 us (1%)
    another operation x25, other arithmetic, factor_inverse(): factor = jnp.linalg.cholesky(gram)  283 us
    another operation x16, other arithmetic, solve_box(): return jax.scipy.linalg.solve_triangular(factor_box, block_box, lower=True)  240 us
    psum x2, waiting for transfers between devices, compress(): gram = lax.psum(partial_gram, 'sample')  67.6 us
    ppermute x2, waiting for transfers between devices, partner(): return lax.ppermute(value, axis, pairs)  28.6 us
  transfers between devices with their start and end apart: 4, of which 4 were waited for; matrix products, arithmetic and copies ran while one was open for 0% of the time, Pallas kernels for 0%

commit v1 on v0

v1 whole, which is shorter than its diff:
```python
import functools
import math

import jax
import jax.numpy as jnp
from jax import lax
from jax.experimental import pallas as pl
from jax.experimental.pallas import tpu as pltpu
from jax.sharding import PartitionSpec as P

SAMPLES = 512
RANK = 128
PANEL = 8
F32 = jnp.float32
BF16 = jnp.bfloat16


def split(value):
    high = value.astype(BF16).astype(F32)
    return high, value - high


def project_kernel(
    distance, group, rows_ref, sketch_ref, z_ref, gram_ref,
    arrived, part, first, partial, second, third,
    row_send, row_recv, first_send, first_recv, second_send, second_recv, third_send, third_recv,
):
    level, sample = lax.axis_index("level"), lax.axis_index("sample")
    upper = level // distance % 2
    other = level + distance - 2 * distance * upper
    core = sample % 2
    mate = sample + 1 - 2 * core
    across = sample + 2 - 4 * (sample // 2 % 2)
    count = arrived.shape[0]
    boxes = count // RANK
    chunks = boxes // group
    half = group // 2

    barrier = pltpu.get_barrier_semaphore()
    for target in ({"level": other}, {"sample": mate}, {"sample": across}):
        pl.semaphore_signal(barrier, inc=1, device_id=target, device_id_type=pl.DeviceIdType.MESH)
    pl.semaphore_wait(barrier, 3)

    def remote(src, dst, send, recv, c, target):
        return pltpu.make_async_remote_copy(
            src_ref=src, dst_ref=dst, send_sem=send.at[c], recv_sem=recv.at[c],
            device_id=target, device_id_type=pl.DeviceIdType.MESH,
        )

    size = group * RANK
    swaps = []
    for c in range(chunks):
        start = pl.multiple_of((1 - upper) * count + c * size, size)
        swap = remote(
            rows_ref.at[pl.ds(start, size)], arrived.at[pl.ds(c * size, size)],
            row_send, row_recv, c, {"level": other},
        )
        swap.start()
        swaps.append(swap)

    left = sketch_ref[:, :RANK].astype(F32)
    right = sketch_ref[:, RANK:].astype(F32)
    with_kept = jnp.where(upper == 1, right, left).astype(BF16)
    with_arrived = jnp.where(upper == 1, left, right).astype(BF16)

    firsts, seconds, thirds = [], [], []

    def compute(c):
        swaps[c].wait_recv()
        for b in range(c * group, (c + 1) * group):
            kept = rows_ref[pl.ds(pl.multiple_of(upper * count + b * RANK, RANK), RANK), :]
            z = jnp.dot(with_kept, kept, preferred_element_type=F32)
            z = z + jnp.dot(with_arrived, arrived[b * RANK:(b + 1) * RANK, :], preferred_element_type=F32)
            z_ref[b] = z
            high, low = split(z)
            high, low = high.astype(BF16), low.astype(BF16)
            part[b] = lax.dot_general(
                jnp.concatenate((high, low, high, low), axis=1),
                jnp.concatenate((high, high, low, low), axis=1),
                (((1,), (1,)), ((), ())), preferred_element_type=F32,
            )
        copy = remote(
            part.at[pl.ds(c * group + (1 - core) * half, half)], first.at[pl.ds(c * half, half)],
            first_send, first_recv, c, {"sample": mate},
        )
        copy.start()
        firsts.append(copy)

    def add_first(c):
        firsts[c].wait_recv()
        for b in range(half):
            partial[c * half + b] = part[c * group + core * half + b] + first[c * half + b]
        copy = remote(
            partial.at[pl.ds(c * half, half)], second.at[pl.ds(c * half, half)],
            second_send, second_recv, c, {"sample": across},
        )
        copy.start()
        seconds.append(copy)

    def add_second(c):
        seconds[c].wait_recv()
        for b in range(half):
            gram_ref[c * group + core * half + b] = partial[c * half + b] + second[c * half + b]
        copy = remote(
            gram_ref.at[pl.ds(c * group + core * half, half)], third.at[pl.ds(c * half, half)],
            third_send, third_recv, c, {"sample": mate},
        )
        copy.start()
        thirds.append(copy)

    def take_third(c):
        thirds[c].wait_recv()
        for b in range(half):
            gram_ref[c * group + (1 - core) * half + b] = third[c * half + b]

    stages = (compute, add_first, add_second, take_third)
    for step in range(chunks + len(stages) - 1):
        for depth, stage in enumerate(stages):
            if 0 <= step - depth < chunks:
                stage(step - depth)
    for copy in swaps + firsts + seconds + thirds:
        copy.wait_send()


def project(rows, sketch_level, distance, group, collective_id):
    count, columns = rows.shape[0] // 2, rows.shape[1]
    boxes = count // RANK
    chunks = boxes // group
    square = (RANK, RANK)
    vmem = pl.BlockSpec(memory_space=pltpu.VMEM)
    return pl.pallas_call(
        functools.partial(project_kernel, distance, group),
        out_shape=(
            jax.ShapeDtypeStruct((boxes, RANK, columns), F32),
            jax.ShapeDtypeStruct((boxes,) + square, F32),
        ),
        in_specs=[vmem, vmem],
        out_specs=(vmem, vmem),
        scratch_shapes=[
            pltpu.VMEM((count, columns), BF16),
            pltpu.VMEM((boxes,) + square, F32),
        ] + [pltpu.VMEM((boxes // 2,) + square, F32)] * 4
        + [pltpu.SemaphoreType.DMA((chunks,))] * 8,
        compiler_params=pltpu.CompilerParams(
            collective_id=collective_id, has_side_effects=True, vmem_limit_bytes=40 * 2**20
        ),
    )(rows, sketch_level)


def factor_kernel(gram_ref, z_ref, factor_ref, rows_ref, work, done):
    boxes, order, _ = gram_ref.shape
    tile = (PANEL, 128)
    lane = lax.broadcasted_iota(jnp.int32, tile, 1)
    row = lax.broadcasted_iota(jnp.int32, tile, 0)
    box_of = lane // PANEL
    unit = (lane % PANEL == row).astype(F32)
    picks = [box_of * PANEL + k for k in range(PANEL)]

    work[:, :, :order] = gram_ref[...]
    work[:, :, order:] = z_ref[...]

    def across_rows(value, j):
        return jnp.broadcast_to(value[j:j + 1, :], (PANEL, value.shape[1]))

    def panel(top, p, carry):
        start = pl.multiple_of(p * PANEL, PANEL)
        packed = unit
        for m in range(boxes):
            shift = lax.rem(m * PANEL + order - p * PANEL, order)
            moved = pltpu.roll(work[m, pl.ds(start, PANEL), :order], shift, axis=1)
            packed = jnp.where(box_of == m, moved, packed)
        column = [jnp.take_along_axis(packed, pick, axis=1) for pick in picks]
        inverse = unit
        for j in range(PANEL):
            scale = lax.rsqrt(across_rows(column[j], j))
            below = column[j] * scale
            for k in range(j + 1, PANEL):
                column[k] = column[k] - below * (across_rows(column[k], j) * scale)
            solved = across_rows(inverse, j) * scale
            inverse = jnp.where(
                row > j, inverse - below * solved, jnp.where(row == j, solved, inverse)
            )
        for m in range(boxes):
            old = work[m, pl.ds(start, PANEL), :]
            new = None
            for k in range(PANEL):
                at = m * PANEL + k
                term = jnp.broadcast_to(inverse[:, at:at + 1], old.shape) * across_rows(old, k)
                new = term if new is None else new + term
            done[m, pl.ds(start, PANEL), :] = new
            high, low = split(new)
            right = jnp.concatenate((high, high, low, low), axis=0).astype(BF16)
            left = jnp.concatenate((high, low, high, low), axis=0)[:, :order]
            left = left.T[top:, :].astype(BF16)
            work[m, top:, :] = work[m, top:, :] - jnp.dot(left, right, preferred_element_type=F32)
        return carry

    strip = 4
    for top in range(0, order // PANEL, strip):
        lax.fori_loop(top, top + strip, functools.partial(panel, top * PANEL), 0)

    keep = lax.broadcasted_iota(jnp.int32, (order, order), 0) >= lax.broadcasted_iota(
        jnp.int32, (order, order), 1
    )

    def finish(m, carry):
        factor_ref[m] = jnp.where(keep, done[m, :, :order].T, 0.0)
        rows_ref[m] = (done[m, :, order:] * math.sqrt(SAMPLES)).astype(rows_ref.dtype)
        return carry

    lax.fori_loop(0, boxes, finish, 0)


def factor(gram, z, dtype):
    boxes, order, columns = z.shape
    together = min(16, boxes)
    spec = pl.BlockSpec((together, order, order), lambda i: (i, 0, 0))
    wide = pl.BlockSpec((together, order, columns), lambda i: (i, 0, 0))
    factors, rows = pl.pallas_call(
        factor_kernel,
        grid=(boxes // together,),
        out_shape=(
            jax.ShapeDtypeStruct((boxes, order, order), F32),
            jax.ShapeDtypeStruct((boxes, order, columns), dtype),
        ),
        in_specs=[spec, wide],
        out_specs=(spec, wide),
        scratch_shapes=[pltpu.VMEM((together, order, order + columns), F32)] * 2,
        compiler_params=pltpu.CompilerParams(vmem_limit_bytes=40 * 2**20),
    )(gram, z)
    return factors, rows.reshape(boxes * order, columns)


def shards(samples, sketch):
    far = lax.axis_size("level") // 2
    z, gram = project(samples, sketch[0], far, 4, 0)
    far_factors, first_rows = factor(gram, z, BF16)
    z, gram = project(first_rows, sketch[1], 1, 2, 1)
    near_factors, basis_rows = factor(gram, z, F32)
    return (far_factors, near_factors, basis_rows)


def solution(mesh):
    return jax.shard_map(
        shards,
        mesh=mesh,
        in_specs=(P("level", "sample"), P()),
        out_specs=(P("level", None, None), P("level", None, None), P("level", "sample")),
        check_vma=False,
    )
```

time: 683 us -> 161 us (0.24)
  other arithmetic: 530 us -> 0 us
  Pallas kernels: 0 us -> 158 us
  waiting for transfers between devices: 96.3 us -> 0 us
  matrix products: 27.2 us -> 0 us
  between operations: 14.7 us -> 0.66 us
    another operation x41 -> x0, other arithmetic: 524 us -> none  [the longest x25 283 us: factor_inverse(): factor = jnp.linalg.cholesky(gram)]
    pallas_call x0 -> x4, Pallas kernels: none -> 158 us  [the longest x2 103 us: factor(): pl.pallas_call(factor_kernel, grid=(boxes // together,), out_shape=(jax.S...]
    psum x2 -> x0, waiting for transfers between devices: 67.6 us -> none  [compress(): gram = lax.psum(partial_gram, 'sample')]
    ppermute x2 -> x0, waiting for transfers between devices: 28.6 us -> none  [partner(): return lax.ppermute(value, axis, pairs)]
    dot_general x32 -> x0, matrix products: 23.2 us -> none  [the longest x24 13 us: batch_product(): jnp.einsum('brs,bst->brt', first, second, precision=lax.Precision.HIGHEST)]
  transfers between devices with their start and end apart: 4 -> 0, of which waited for: 4 -> 0; matrix products, arithmetic and copies ran while one was open for 0% -> 0% of each run, Pallas kernels for 0% -> 0%
where the time goes in v1:
time: 161 us
  Pallas kernels  158 us (98%)
  local copies, waits for them, and re-layouts  2.1 us (1%)
    pallas_call x2, Pallas kernels, factor(): pl.pallas_call(factor_kernel, grid=(boxes // together,), out_shape=(jax.S...  103 us
    pallas_call x2, Pallas kernels, project(): pl.pallas_call(functools.partial(project_kernel, distance, group), out_sh...  55.2 us

profile of v1, /device:TPU:0, one launch (start us, length us, event | category | flops | bytes accessed | tf_op | source)
XLA Modules:
  0.0 160.6 jit_solution(9920015883838841325)
XLA Ops:
  0.6 0.9 slice_bitcast_fusion
  1.5 0.0 copy-start
  1.5 1.2 copy-done
  2.7 38.1 %shard_map.49 = (f32[16,128,128]{2,1,0:T(8,128)S(1)}, f32[16,128,128]{2,1,0:T(8,128)S(1)}) custom-call(bf16[4096,128]{1,0:T(8,128)(2,1)S(1)} %copy-done, bf16[128,256]{1,0:T(8,128)(2,1)S(1)} %get-tuple-element.20.sketch_ref), custom_call_target="tpu_custom_call" | custom-call | tf_op jit(solution)/shard_map/pallas_call | solution.py:131
  40.8 66.7 %shard_map.50 = (f32[16,128,128]{2,1,0:T(8,128)}, bf16[16,128,128]{2,1,0:T(8,128)(2,1)S(1)}) custom-call(f32[16,128,128]{2,1,0:T(8,128)S(1)} %get-tuple-element.11.gram_ref, f32[16,128,128]{2,1,0:T(8,128)S(1)} %get-tuple-element.12.z_ref), custom_call_target="tpu_custom_call" | custom-call | tf_op jit(solution)/shard_map/pallas_call | solution.py:219
  107.5 17.1 %shard_map.51 = (f32[8,128,128]{2,1,0:T(8,128)S(1)}, f32[8,128,128]{2,1,0:T(8,128)S(1)}) custom-call(bf16[2048,128]{1,0:T(8,128)(2,1)S(1)} %bitcast.6, bf16[128,256]{1,0:T(8,128)(2,1)S(1)} %get-tuple-element.19.sketch_ref), custom_call_target="tpu_custom_call" | custom-call | tf_op jit(solution)/shard_map/pallas_call | solution.py:131
  124.7 36.0 %shard_map.52 = (f32[8,128,128]{2,1,0:T(8,128)}, f32[8,128,128]{2,1,0:T(8,128)}) custom-call(f32[8,128,128]{2,1,0:T(8,128)S(1)} %get-tuple-element.15.gram_ref, f32[8,128,128]{2,1,0:T(8,128)S(1)} %get-tuple-element.16.z_ref), custom_call_target="tpu_custom_call" | custom-call | tf_op jit(solution)/shard_map/pallas_call | solution.py:219
Async XLA Ops:
  1.5 1.2 copy-start
